TPU v7x, 256 devices: a whole 4x4x8 slice. The times are simulated.
256 devices in a mesh: dp: 32 (over y, x, z_hi), section: 4 (over z_lo), tensor: 2 (over core).
Axes of the slice: x: 4, y: 4, z: 8 (z_hi: 2, z_lo: 4; z = z_hi * 4 + z_lo), core: 2. Of those that a mesh axis runs over, the one named last changes fastest.
Arguments:
- tokens_in: bfloat16 [4096, 3584], P('dp', 'tensor'), may hold values from -8 to 8
- query_gain: float32 [4, 3584], P('section', 'tensor'), may hold values from -1.5 to 1.5
- key_gain: float32 [4, 3584], P('section', 'tensor'), may hold values from -1.5 to 1.5
- value_gain: float32 [4, 3584], P('section', 'tensor'), may hold values from 0.5 to 2
- out_weight: bfloat16 [4, 3584, 3584], P('section', 'tensor', 'dp'), may hold values from -0.1875 to 0.1875
- doc_lengths: int32 [32, 4], P('dp'), may hold values from 1 to 64, 128 in all within a row
- grad_out: bfloat16 [4096, 3584], P('dp', 'tensor'), may hold values from -6 to 6
Outputs:
- layer_outputs: bfloat16 [4, 4096, 3584], P('section', 'dp', 'tensor')
- input_grads: bfloat16 [4, 4096, 3584], P('section', 'dp', 'tensor')
- weight_grads: float32 [4, 3584, 3584], P('section', 'tensor', 'dp')
Inputs may be any that keep to these rules, and one draw needn't show every extreme that they name: `doc_lengths`: each row sums to 128; the longest document of every row has exactly 64 tokens.
All inputs are finite; a program needn't handle non-finite values.
Results may differ from a plain program's by a relative error of at most 0.035.
Values may be sent and summed in bfloat16 or wider, within the bound.
No kernel may reach another device: no remote copies, remote signals or barrier semaphores. Data moves between devices by JAX's collectives and lax.ppermute only.
A program may use at most 128 MiB of HBM per device.

v0:
```python
import math

import jax
import jax.numpy as jnp
from jax import lax
from jax.sharding import PartitionSpec as P

HEAD_DIM = 128
GROUPS = 8


EPS = 1e-05


def passed_along(block, axis, distance):
    devices = range(lax.axis_size(axis))
    route = [(i - distance, i) for i in devices if i - distance in devices]
    return lax.ppermute(block, axis, route)


def doc_mask(lengths, count):
    ends = jnp.cumsum(lengths)
    places = jnp.arange(count, dtype=jnp.int32)
    ident = jnp.sum((places[:, None] >= ends[None, :]).astype(jnp.int32), axis=1)
    causal = places[None, :] <= places[:, None]
    return causal & (ident[:, None] == ident[None, :])


def attend_exact(query_src, key_src, gains, allowed):
    rows_q = query_src.shape[0]
    rows_k = key_src.shape[0]
    queries = (query_src * gains[0]).reshape(rows_q, -1, HEAD_DIM)
    keys = (key_src * gains[1]).reshape(rows_k, -1, HEAD_DIM)
    values = (key_src * gains[2]).reshape(rows_k, -1, HEAD_DIM)
    scores = jnp.einsum("qhd,khd->hqk", queries, keys, precision=lax.Precision.HIGHEST) / jnp.sqrt(
        jnp.float32(HEAD_DIM)
    )
    scores = jnp.where(allowed[None], scores, -1e30)
    top = lax.stop_gradient(jnp.max(scores, axis=-1, keepdims=True))
    expo = jnp.exp(scores - top)
    probs = expo / jnp.sum(expo, axis=-1, keepdims=True)
    mixed = jnp.einsum("hqk,khd->qhd", probs, values, precision=lax.Precision.HIGHEST)
    return mixed.reshape(rows_q, -1)


def local(tokens_in, query_gain, key_gain, value_gain, out_weight, doc_lengths, grad_out):
    seq_len = tokens_in.shape[0]
    local_width = tokens_in.shape[1]
    full_width = local_width * lax.axis_size("tensor")
    heads_local = local_width // HEAD_DIM
    section_count = lax.axis_size("section")
    section_pos = lax.axis_index("section")
    block_rows = seq_len // GROUPS
    block_count = seq_len // block_rows
    turns = section_count + block_count - 1
    score_scale = 1.0 / math.sqrt(HEAD_DIM)
    weights_full = lax.all_gather(out_weight[0], "dp", axis=1, tiled=True)
    gains = (query_gain[0], key_gain[0], value_gain[0])
    allowed = doc_mask(doc_lengths[0], seq_len)

    def place(buffer, piece, row_start, is_valid):
        return jnp.where(
            is_valid, lax.dynamic_update_slice_in_dim(buffer, piece, row_start, 0), buffer
        )

    def forward_turn(turn, carry):
        inputs_buf, norms_buf, keys_buf, values_buf, attn_buf, outputs_buf, arrived = carry
        group_pos = turn - section_pos
        is_valid = (group_pos >= 0) & (group_pos < block_count)
        row_start = jnp.clip(group_pos, 0, block_count - 1) * block_rows
        own_rows = lax.dynamic_slice_in_dim(tokens_in, row_start, block_rows, 0)
        group_in = jnp.where(section_pos == 0, own_rows, arrived)
        group_f = group_in.astype(jnp.float32)
        squares = lax.psum(jnp.sum(group_f * group_f, axis=1), "tensor")
        inverse = lax.rsqrt(squares / full_width + EPS)
        normed = group_f * inverse[:, None]
        queries = (normed * gains[0]).astype(jnp.bfloat16)
        keys_new = (normed * gains[1]).astype(jnp.bfloat16)
        values_new = (normed * gains[2]).astype(jnp.bfloat16)
        keys_buf = place(keys_buf, keys_new, row_start, is_valid)
        values_buf = place(values_buf, values_new, row_start, is_valid)
        rows_mask = lax.dynamic_slice_in_dim(allowed, row_start, block_rows, 0)
        query_heads = queries.reshape(block_rows, heads_local, HEAD_DIM)
        key_heads = keys_buf.reshape(seq_len, heads_local, HEAD_DIM)
        value_heads = values_buf.reshape(seq_len, heads_local, HEAD_DIM)
        scores = (
            jnp.einsum("qhd,khd->hqk", query_heads, key_heads, preferred_element_type=jnp.float32)
            * score_scale
        )
        scores = jnp.where(rows_mask[None], scores, -1e30)
        top = jnp.max(scores, axis=-1, keepdims=True)
        expo = jnp.exp(scores - top)
        probs = (expo / jnp.sum(expo, axis=-1, keepdims=True)).astype(jnp.bfloat16)
        mixed = jnp.einsum("hqk,khd->qhd", probs, value_heads, preferred_element_type=jnp.float32)
        mixed = mixed.astype(jnp.bfloat16).reshape(block_rows, local_width)
        partial_value = jnp.dot(mixed, weights_full, preferred_element_type=jnp.float32)
        summed = lax.psum_scatter(
            partial_value.astype(jnp.bfloat16), "tensor", scatter_dimension=1, tiled=True
        ).astype(jnp.float32)
        group_out = (group_f + summed).astype(jnp.bfloat16)
        inputs_buf = place(inputs_buf, group_in, row_start, is_valid)
        norms_buf = place(norms_buf, inverse, row_start, is_valid)
        attn_buf = place(attn_buf, mixed, row_start, is_valid)
        outputs_buf = place(outputs_buf, group_out, row_start, is_valid)
        arrived = passed_along(group_out, "section", 1)
        return (inputs_buf, norms_buf, keys_buf, values_buf, attn_buf, outputs_buf, arrived)

    empty_rows = jnp.zeros((seq_len, local_width), jnp.bfloat16)
    start_fwd = (
        empty_rows,
        jnp.zeros((seq_len,), jnp.float32),
        empty_rows,
        empty_rows,
        empty_rows,
        empty_rows,
        jnp.zeros((block_rows, local_width), jnp.bfloat16),
    )
    inputs_buf, norms_buf, keys_buf, values_buf, attn_buf, outputs_buf, arrived = lax.fori_loop(
        0, turns, forward_turn, start_fwd
    )
    normed_all = inputs_buf.astype(jnp.float32) * norms_buf[:, None]

    def backward_turn(turn, carry):
        grads_buf, dnormed_buf, grad_all_buf, arrived_grad = carry
        back_pos = turn - (section_count - 1 - section_pos)
        is_valid = (back_pos >= 0) & (back_pos < block_count)
        group_pos = block_count - 1 - back_pos
        row_start = jnp.clip(group_pos, 0, block_count - 1) * block_rows
        own_rows = lax.dynamic_slice_in_dim(grad_out, row_start, block_rows, 0)
        grad_group = jnp.where(section_pos == section_count - 1, own_rows, arrived_grad)
        grad_full = lax.all_gather(grad_group, "tensor", axis=1, tiled=True)
        grad_mixed = lax.dot_general(
            grad_full, weights_full, (((1,), (1,)), ((), ())), preferred_element_type=jnp.float32
        )
        normed_rows = lax.dynamic_slice_in_dim(normed_all, row_start, block_rows, 0)
        rows_mask = lax.dynamic_slice_in_dim(allowed, row_start, block_rows, 0)
        _, pull = jax.vjp(
            lambda query_src, key_src: attend_exact(query_src, key_src, gains, rows_mask),
            normed_rows,
            normed_all,
        )
        grad_rows, grad_keys = pull(grad_mixed)
        updated = dnormed_buf + grad_keys
        updated = lax.dynamic_update_slice_in_dim(
            updated,
            lax.dynamic_slice_in_dim(updated, row_start, block_rows, 0) + grad_rows,
            row_start,
            0,
        )
        dnormed_buf = jnp.where(is_valid, updated, dnormed_buf)
        grad_normed = lax.dynamic_slice_in_dim(dnormed_buf, row_start, block_rows, 0)
        inputs_rows = lax.dynamic_slice_in_dim(inputs_buf, row_start, block_rows, 0).astype(
            jnp.float32
        )
        inverse = lax.dynamic_slice_in_dim(norms_buf, row_start, block_rows, 0)
        grad_inverse = lax.psum(jnp.sum(grad_normed * inputs_rows, axis=1), "tensor")
        grad_in = (
            grad_group.astype(jnp.float32)
            + grad_normed * inverse[:, None]
            - inputs_rows * (grad_inverse * inverse * inverse * inverse / full_width)[:, None]
        )
        grad_in = grad_in.astype(jnp.bfloat16)
        grads_buf = place(grads_buf, grad_in, row_start, is_valid)
        grad_all_buf = place(grad_all_buf, grad_full, row_start, is_valid)
        arrived_grad = passed_along(grad_in, "section", -1)
        return (grads_buf, dnormed_buf, grad_all_buf, arrived_grad)

    start_bwd = (
        empty_rows,
        jnp.zeros((seq_len, local_width), jnp.float32),
        jnp.zeros((seq_len, full_width), jnp.bfloat16),
        jnp.zeros((block_rows, local_width), jnp.bfloat16),
    )
    grads_buf, dnormed_buf, grad_all_buf, arrived_grad = lax.fori_loop(
        0, turns, backward_turn, start_bwd
    )
    weight_term = lax.dot_general(
        attn_buf, grad_all_buf, (((0,), (0,)), ((), ())), preferred_element_type=jnp.float32
    )
    weight_grads = lax.psum_scatter(
        weight_term.astype(jnp.bfloat16), "dp", scatter_dimension=1, tiled=True
    ).astype(jnp.float32)
    return (outputs_buf[None], grads_buf[None], weight_grads[None])


def solution(mesh):
    return jax.shard_map(
        local,
        mesh=mesh,
        in_specs=(
            P("dp", "tensor"),
            P("section", "tensor"),
            P("section", "tensor"),
            P("section", "tensor"),
            P("section", "tensor", "dp"),
            P("dp", None),
            P("dp", "tensor"),
        ),
        out_specs=(
            P("section", "dp", "tensor"),
            P("section", "dp", "tensor"),
            P("section", "tensor", "dp"),
        ),
        check_vma=False,
    )
```

profile of v0, /device:TPU:32, one launch (start us, length us, event | category | flops | bytes accessed | tf_op | source)
XLA Modules:
  0.0 1975.4 jit_solution(15948075492809810235)
XLA Ops:
  11.5 203.1 %all-gather.3.cloned.1.call-done = bf16[1,1792,3584]{1,2,0:T(8,128)(2,1)} async-done(((bf16[1,1792,112]{1,2,0:T(8,128)(2,1)}), bf16[1,1792,3584]{1,2,0:T(8,128)(2,1)}) %all-gather.3.cloned.1.call-update) | async-done | bytes 12845072 | tf_op jit(solution)/shard_map/all_gather | solution.py:57
  214.6 18.0 copy.171
  234.1 501.5 %while.48 = (s32[]{:T(128)}, bf16[128,1792]{1,0:T(8,128)(2,1)S(1)}, f32[128]{0:T(128)}, bf16[128,1792]{1,0:T(8,128)(2,1)S(1)}, bf16[128,1792]{1,0:T(8,128)(2,1)S...) while((s32[]{:T(128)}, bf16[128,1792]{1,0:T(8,128)(2,1)S(1)}, ...), condition=%wide.region_8.9_spmd, body=%wide.region_2.8_spmd.sunk | while | flops 221147680 | bytes 20374132 | solution.py:118
  249.0 7.1 convolution_convert_fusion.4
  256.1 9.3 reduce-scatter.5.cloned.1.call-done
  287.9 7.1 convolution_convert_fusion.4
  295.0 15.9 reduce-scatter.5.cloned.1.call-done
  336.7 7.1 convolution_convert_fusion.4
  343.8 13.4 reduce-scatter.5.cloned.1.call-done
  383.0 7.1 convolution_convert_fusion.4
  390.2 13.4 reduce-scatter.5.cloned.1.call-done
  429.4 7.1 convolution_convert_fusion.4
  436.5 13.4 reduce-scatter.5.cloned.1.call-done
  475.7 7.1 convolution_convert_fusion.4
  482.9 13.4 reduce-scatter.5.cloned.1.call-done
  522.1 7.1 convolution_convert_fusion.4
  529.2 13.4 reduce-scatter.5.cloned.1.call-done
  568.4 7.1 convolution_convert_fusion.4
  575.6 13.4 reduce-scatter.5.cloned.1.call-done
  614.8 7.1 convolution_convert_fusion.4
  621.9 13.4 reduce-scatter.5.cloned.1.call-done
  668.2 13.4 reduce-scatter.5.cloned.1.call-done
  714.6 13.4 reduce-scatter.5.cloned.1.call-done
  739.4 662.3 %while.49 = (s32[]{:T(128)}, bf16[128,1792]{0,1:T(8,128)(2,1)}, f32[128,1792]{0,1:T(8,128)}, bf16[128,3584]{0,1:T(8,128)(2,1)}, bf16[16,1792]{0,1:T(8,128)(2,1)S...) while((s32[]{:T(128)}, bf16[128,1792]{0,1:T(8,128)(2,1)}, ...), condition=%wide.region_15.16_spmd.clone, body=%wide.region_9.15_spmd.clone.sunk | while | flops 429191232 | bytes 46234376 | solution.py:174
  746.4 8.0 fusion.116
  789.1 9.7 select_n.339
  806.2 8.0 fusion.116
  848.8 9.7 select_n.339
  865.9 8.0 fusion.116
  909.7 9.7 select_n.339
  926.9 8.0 fusion.116
  970.7 9.7 select_n.339
  987.8 8.0 fusion.116
  1031.6 9.7 select_n.339
  1048.7 8.0 fusion.116
  1092.5 9.7 select_n.339
  1109.7 8.0 fusion.116
  1153.5 9.7 select_n.339
  1170.6 8.0 fusion.116
  1214.4 9.7 select_n.339
  1231.5 8.0 fusion.116
  1275.4 9.7 select_n.339
  1292.5 8.0 fusion.116
  1335.4 8.3 select_n.339
  1351.1 8.0 fusion.116
  1392.9 8.3 select_n.339
  1401.6 9.4 convolution_convert_fusion.2
  1412.1 554.8 %reduce-scatter.3.cloned.1.call-done = bf16[1792,112]{0,1:T(8,128)(2,1)} async-done(((bf16[1792,3584]{0,1:T(8,128)(2,1)}), bf16[1792,112]{0,1:T(8,128)(2,1)}) %reduce-scatter.3.cloned.1.call-update) | async-done | bytes 401424 | tf_op jit(solution)/shard_map/reduce_scatter | solution.py:180
  (755 shorter events, 770.4 us)
Async XLA Ops:
  7.2 207.5 %all-gather.3.cloned.1.call-start = ((), (), s32[]{:S(2)}) async-start(), calls=%async_computation.3 | async-start | bytes 13246464 | tf_op jit(solution)/shard_map/all_gather | solution.py:57
  234.1 31.3 %reduce-scatter.5.cloned.1.call-start = ((), (), s32[]{:S(2)}) async-start(), calls=%async_computation.4 | async-start | bytes 172032 | tf_op jit(solution)/shard_map/while/body/eval_jaxpr/reduce_scatter | solution.py:97
  266.9 6.1 collective-permute-start
  273.0 37.9 %reduce-scatter.5.cloned.1.call-start = ((), (), s32[]{:S(2)}) async-start(), calls=%async_computation.4 | async-start | bytes 172032 | tf_op jit(solution)/shard_map/while/body/eval_jaxpr/reduce_scatter | solution.py:97
  312.4 6.1 collective-permute-start
  318.5 38.8 %reduce-scatter.5.cloned.1.call-start = ((), (), s32[]{:S(2)}) async-start(), calls=%async_computation.4 | async-start | bytes 172032 | tf_op jit(solution)/shard_map/while/body/eval_jaxpr/reduce_scatter | solution.py:97
  358.8 6.1 collective-permute-start
  364.8 38.8 %reduce-scatter.5.cloned.1.call-start = ((), (), s32[]{:S(2)}) async-start(), calls=%async_computation.4 | async-start | bytes 172032 | tf_op jit(solution)/shard_map/while/body/eval_jaxpr/reduce_scatter | solution.py:97
  405.1 6.1 collective-permute-start
  411.2 38.8 %reduce-scatter.5.cloned.1.call-start = ((), (), s32[]{:S(2)}) async-start(), calls=%async_computation.4 | async-start | bytes 172032 | tf_op jit(solution)/shard_map/while/body/eval_jaxpr/reduce_scatter | solution.py:97
  451.5 6.1 collective-permute-start
  457.5 38.8 %reduce-scatter.5.cloned.1.call-start = ((), (), s32[]{:S(2)}) async-start(), calls=%async_computation.4 | async-start | bytes 172032 | tf_op jit(solution)/shard_map/while/body/eval_jaxpr/reduce_scatter | solution.py:97
  497.8 6.1 collective-permute-start
  503.9 38.8 %reduce-scatter.5.cloned.1.call-start = ((), (), s32[]{:S(2)}) async-start(), calls=%async_computation.4 | async-start | bytes 172032 | tf_op jit(solution)/shard_map/while/body/eval_jaxpr/reduce_scatter | solution.py:97
  544.1 6.1 collective-permute-start
  550.2 38.8 %reduce-scatter.5.cloned.1.call-start = ((), (), s32[]{:S(2)}) async-start(), calls=%async_computation.4 | async-start | bytes 172032 | tf_op jit(solution)/shard_map/while/body/eval_jaxpr/reduce_scatter | solution.py:97
  590.5 6.1 collective-permute-start
  596.6 38.8 %reduce-scatter.5.cloned.1.call-start = ((), (), s32[]{:S(2)}) async-start(), calls=%async_computation.4 | async-start | bytes 172032 | tf_op jit(solution)/shard_map/while/body/eval_jaxpr/reduce_scatter | solution.py:97
  636.9 6.1 collective-permute-start
  642.9 38.8 %reduce-scatter.5.cloned.1.call-start = ((), (), s32[]{:S(2)}) async-start(), calls=%async_computation.4 | async-start | bytes 172032 | tf_op jit(solution)/shard_map/while/body/eval_jaxpr/reduce_scatter | solution.py:97
  683.2 6.1 collective-permute-start
  689.3 38.8 %reduce-scatter.5.cloned.1.call-start = ((), (), s32[]{:S(2)}) async-start(), calls=%async_computation.4 | async-start | bytes 172032 | tf_op jit(solution)/shard_map/while/body/eval_jaxpr/reduce_scatter | solution.py:97
  729.5 6.1 collective-permute-start
  735.6 0.8 copy-start.2
  735.6 1231.4 %reduce-scatter.3.cloned.1.call-start = ((), (), s32[]{:S(2)}) async-start(), calls=%async_computation.2 | async-start | bytes 13246464 | tf_op jit(solution)/shard_map/reduce_scatter | solution.py:180
  739.7 15.6 copy-start
  777.9 20.9 %collective-permute-start.1 = (bf16[16,1792]{1,0:T(8,128)(2,1)}, bf16[16,1792]{1,0:T(8,128)(2,1)S(1)}, u32[]{:S(2)}, u32[]{:S(2)}) collective-permute-start(bf16[16,1792]{1,0:T(8,128)(2,1)} %get-tuple-element.1264), channel_id=1, source_target_pairs={{2,0},{4,2},{6,4},{3,1},{5,3},{7,5},{10,8},{12,10},{14,12},{11,9},... | collective-permute-start | bytes 172040 | tf_op jit(solution)/shard_map/while/body/eval_jaxpr/ppermute | solution.py:18
  799.4 15.6 copy-start
  837.7 20.9 %collective-permute-start.1 = (bf16[16,1792]{1,0:T(8,128)(2,1)}, bf16[16,1792]{1,0:T(8,128)(2,1)S(1)}, u32[]{:S(2)}, u32[]{:S(2)}) collective-permute-start(bf16[16,1792]{1,0:T(8,128)(2,1)} %get-tuple-element.1264), channel_id=1, source_target_pairs={{2,0},{4,2},{6,4},{3,1},{5,3},{7,5},{10,8},{12,10},{14,12},{11,9},... | collective-permute-start | bytes 172040 | tf_op jit(solution)/shard_map/while/body/eval_jaxpr/ppermute | solution.py:18
  859.1 15.6 copy-start
  898.6 20.9 %collective-permute-start.1 = (bf16[16,1792]{1,0:T(8,128)(2,1)}, bf16[16,1792]{1,0:T(8,128)(2,1)S(1)}, u32[]{:S(2)}, u32[]{:S(2)}) collective-permute-start(bf16[16,1792]{1,0:T(8,128)(2,1)} %get-tuple-element.1264), channel_id=1, source_target_pairs={{2,0},{4,2},{6,4},{3,1},{5,3},{7,5},{10,8},{12,10},{14,12},{11,9},... | collective-permute-start | bytes 172040 | tf_op jit(solution)/shard_map/while/body/eval_jaxpr/ppermute | solution.py:18
  920.1 15.6 copy-start
  959.5 20.9 %collective-permute-start.1 = (bf16[16,1792]{1,0:T(8,128)(2,1)}, bf16[16,1792]{1,0:T(8,128)(2,1)S(1)}, u32[]{:S(2)}, u32[]{:S(2)}) collective-permute-start(bf16[16,1792]{1,0:T(8,128)(2,1)} %get-tuple-element.1264), channel_id=1, source_target_pairs={{2,0},{4,2},{6,4},{3,1},{5,3},{7,5},{10,8},{12,10},{14,12},{11,9},... | collective-permute-start | bytes 172040 | tf_op jit(solution)/shard_map/while/body/eval_jaxpr/ppermute | solution.py:18
  981.0 15.6 copy-start
  1020.5 20.9 %collective-permute-start.1 = (bf16[16,1792]{1,0:T(8,128)(2,1)}, bf16[16,1792]{1,0:T(8,128)(2,1)S(1)}, u32[]{:S(2)}, u32[]{:S(2)}) collective-permute-start(bf16[16,1792]{1,0:T(8,128)(2,1)} %get-tuple-element.1264), channel_id=1, source_target_pairs={{2,0},{4,2},{6,4},{3,1},{5,3},{7,5},{10,8},{12,10},{14,12},{11,9},... | collective-permute-start | bytes 172040 | tf_op jit(solution)/shard_map/while/body/eval_jaxpr/ppermute | solution.py:18
  1041.9 15.6 copy-start
  1081.4 20.9 %collective-permute-start.1 = (bf16[16,1792]{1,0:T(8,128)(2,1)}, bf16[16,1792]{1,0:T(8,128)(2,1)S(1)}, u32[]{:S(2)}, u32[]{:S(2)}) collective-permute-start(bf16[16,1792]{1,0:T(8,128)(2,1)} %get-tuple-element.1264), channel_id=1, source_target_pairs={{2,0},{4,2},{6,4},{3,1},{5,3},{7,5},{10,8},{12,10},{14,12},{11,9},... | collective-permute-start | bytes 172040 | tf_op jit(solution)/shard_map/while/body/eval_jaxpr/ppermute | solution.py:18
  1102.9 15.6 copy-start
  1142.3 20.9 %collective-permute-start.1 = (bf16[16,1792]{1,0:T(8,128)(2,1)}, bf16[16,1792]{1,0:T(8,128)(2,1)S(1)}, u32[]{:S(2)}, u32[]{:S(2)}) collective-permute-start(bf16[16,1792]{1,0:T(8,128)(2,1)} %get-tuple-element.1264), channel_id=1, source_target_pairs={{2,0},{4,2},{6,4},{3,1},{5,3},{7,5},{10,8},{12,10},{14,12},{11,9},... | collective-permute-start | bytes 172040 | tf_op jit(solution)/shard_map/while/body/eval_jaxpr/ppermute | solution.py:18
  1163.8 15.6 copy-start
  1203.3 20.9 %collective-permute-start.1 = (bf16[16,1792]{1,0:T(8,128)(2,1)}, bf16[16,1792]{1,0:T(8,128)(2,1)S(1)}, u32[]{:S(2)}, u32[]{:S(2)}) collective-permute-start(bf16[16,1792]{1,0:T(8,128)(2,1)} %get-tuple-element.1264), channel_id=1, source_target_pairs={{2,0},{4,2},{6,4},{3,1},{5,3},{7,5},{10,8},{12,10},{14,12},{11,9},... | collective-permute-start | bytes 172040 | tf_op jit(solution)/shard_map/while/body/eval_jaxpr/ppermute | solution.py:18
  1224.7 15.6 copy-start
  1264.2 20.9 %collective-permute-start.1 = (bf16[16,1792]{1,0:T(8,128)(2,1)}, bf16[16,1792]{1,0:T(8,128)(2,1)S(1)}, u32[]{:S(2)}, u32[]{:S(2)}) collective-permute-start(bf16[16,1792]{1,0:T(8,128)(2,1)} %get-tuple-element.1264), channel_id=1, source_target_pairs={{2,0},{4,2},{6,4},{3,1},{5,3},{7,5},{10,8},{12,10},{14,12},{11,9},... | collective-permute-start | bytes 172040 | tf_op jit(solution)/shard_map/while/body/eval_jaxpr/ppermute | solution.py:18
  1285.7 15.6 copy-start
  1325.1 18.6 collective-permute-start.1
  1344.3 15.6 copy-start
  1382.6 18.6 collective-permute-start.1
  1401.6 9.5 copy-start.1
Sparse Core Ops, SparseCore 0:
  11.4 203.1 all-gather.2
  256.2 9.1 reduce-scatter.4
  295.2 15.7 reduce-scatter.4
  343.9 13.2 reduce-scatter.4
  390.3 13.2 reduce-scatter.4
  436.6 13.2 reduce-scatter.4
  483.0 13.2 reduce-scatter.4
  529.3 13.2 reduce-scatter.4
  575.7 13.2 reduce-scatter.4
  622.0 13.2 reduce-scatter.4
  668.4 13.2 reduce-scatter.4
  714.7 13.2 reduce-scatter.4
  1411.2 555.6 reduce-scatter.2
where the time goes:
time: 1990 us; the launch traced here: 1980 us
  waiting for transfers between devices  928 us (47%)
  local copies, waits for them, and re-layouts  426 us (21%)
  matrix products  280 us (14%)
  other arithmetic  189 us (9%)
  blocking collectives  75 us (4%)
  starting transfers between devices  59.1 us (3%)
    reduce_scatter x1, waiting for transfers between devices, local(): lax.psum_scatter(weight_term.astype(jnp.bfloat16), 'dp', scatter_dimensio...  555 us
    select_n x88, local copies, waits for them, and re-layouts, place(): jnp.where(is_valid, lax.dynamic_update_slice_in_dim(buffer, piece, row_st...  265 us
    all_gather x1, waiting for transfers between devices, local(): weights_full = lax.all_gather(out_weight[0], 'dp', axis=1, tiled=True)  203 us
    reduce_scatter x11, waiting for transfers between devices, forward_turn(): lax.psum_scatter(partial_value.astype(jnp.bfloat16), 'tensor', scatter_di...  146 us
    while x121, local copies, waits for them, and re-layouts  92.7 us
    dot_general x11, matrix products, backward_turn(): lax.dot_general(grad_full, weights_full, (((1,), (1,)), ((), ())), prefer...  88.4 us
    dot_general x11, matrix products, forward_turn(): jnp.dot(mixed, weights_full, preferred_element_type=jnp.float32)  78.1 us
    dot_general x33, matrix products, attend_exact(): jnp.einsum('qhd,khd->hqk', queries, keys, precision=lax.Precision.HIGHEST)  66.3 us
  transfers between devices with their start and end apart: 35, of which 24 were waited for; matrix products, arithmetic and copies ran while one was open for 11% of the time, Pallas kernels for 0%

commit v1 on v0

v1 whole, which is shorter than its diff:
```python
import jax
import jax.numpy as jnp
from jax import lax
from jax.experimental import pallas as pl
from jax.experimental.pallas import tpu as pltpu
from jax.sharding import PartitionSpec as P

HEAD_DIM = 128
EPS = 1e-05
CHUNK = 256
F32 = jnp.float32
BF16 = jnp.bfloat16
NN = (((1,), (0,)), ((), ()))
NT = (((1,), (1,)), ((), ()))
TN = (((0,), (0,)), ((), ()))
VMEM_LIMIT = 48 * 1024 * 1024


def dot(a, b, dims):
    return lax.dot_general(a, b, dims, preferred_element_type=F32)


def split(a):
    high = a.astype(BF16)
    return high, (a - high.astype(F32)).astype(BF16)


def weight_copies(half, weight_ref, held, sems):
    rows, width = held.shape
    copies = []
    for i in range(rows // CHUNK):
        source = lax.rem(half * width + i * CHUNK, rows)
        source = pl.multiple_of(source, CHUNK)
        copies.append(
            pltpu.make_async_copy(
                weight_ref.at[pl.ds(source, CHUNK)], held.at[pl.ds(i * CHUNK, CHUNK)], sems.at[i]
            )
        )
    return copies


def allowed_mask(id_col, id_row):
    shape = (id_col.shape[0], id_row.shape[1])
    rows = lax.broadcasted_iota(jnp.int32, shape, 0)
    cols = lax.broadcasted_iota(jnp.int32, shape, 1)
    return (rows >= cols) & (id_col[...] == id_row[...])


def forward_kernel(
    half_ref, x_ref, squares_ref, gq_ref, gk_ref, gv_ref, id_col, id_row, weight_ref,
    own_ref, other_ref, mixed_ref, held, sems,
):
    copies = weight_copies(half_ref[0], weight_ref, held, sems)
    for copy in copies:
        copy.start()
    width = x_ref.shape[1]
    inverse = lax.rsqrt(squares_ref[...] / (2 * width) + EPS)
    allowed = allowed_mask(id_col, id_row)
    scale = HEAD_DIM**-0.5
    for head in range(width // HEAD_DIM):
        cols = slice(head * HEAD_DIM, (head + 1) * HEAD_DIM)
        normed = x_ref[:, cols].astype(F32) * inverse
        queries = (normed * gq_ref[:, cols]).astype(BF16)
        keys = (normed * gk_ref[:, cols]).astype(BF16)
        values = (normed * gv_ref[:, cols]).astype(BF16)
        scores = jnp.where(allowed, dot(queries, keys, NT) * scale, -1e30)
        expo = jnp.exp(scores - jnp.max(scores, axis=1, keepdims=True))
        probs = (expo / jnp.sum(expo, axis=1, keepdims=True)).astype(BF16)
        mixed_ref[:, cols] = dot(probs, values, NN).astype(BF16)
    mixed = mixed_ref[...]
    per_half = width // CHUNK
    for i, copy in enumerate(copies):
        copy.wait()
        piece = dot(mixed, held[i * CHUNK : (i + 1) * CHUNK], NT).astype(BF16)
        target = own_ref if i < per_half else other_ref
        start = (i % per_half) * CHUNK
        target[:, start : start + CHUNK] = piece


def backward_kernel(
    half_ref, x_ref, squares_ref, gq_ref, gk_ref, gv_ref, id_col, id_row, weight_ref,
    grad_ref, grad_other_ref, sum_ref, inner_ref, held, probs_buf, sems,
):
    copies = weight_copies(half_ref[0], weight_ref, held, sems)
    for copy in copies:
        copy.start()
    width = x_ref.shape[1]
    heads = width // HEAD_DIM
    inverse = lax.rsqrt(squares_ref[...] / (2 * width) + EPS)
    allowed = allowed_mask(id_col, id_row)
    scale = HEAD_DIM**-0.5
    for head in range(heads):
        cols = slice(head * HEAD_DIM, (head + 1) * HEAD_DIM)
        normed = x_ref[:, cols].astype(F32) * inverse
        q_high, q_low = split(normed * gq_ref[:, cols])
        k_high, k_low = split(normed * gk_ref[:, cols])
        scores = dot(
            jnp.concatenate([q_high, q_high, q_low], axis=1),
            jnp.concatenate([k_high, k_low, k_high], axis=1),
            NT,
        )
        scores = jnp.where(allowed, scores * scale, -1e30)
        expo = jnp.exp(scores - jnp.max(scores, axis=1, keepdims=True))
        probs_buf[head] = expo / jnp.sum(expo, axis=1, keepdims=True)
    for copy in copies:
        copy.wait()
    inner = jnp.zeros((x_ref.shape[0], HEAD_DIM), F32)
    for pair in range(width // CHUNK):
        wide = slice(pair * CHUNK, (pair + 1) * CHUNK)
        grad_mixed = dot(grad_ref[...], held[:width, wide], NN) + dot(
            grad_other_ref[...], held[width:, wide], NN
        )
        for part in range(CHUNK // HEAD_DIM):
            head = pair * (CHUNK // HEAD_DIM) + part
            cols = slice(head * HEAD_DIM, (head + 1) * HEAD_DIM)
            grad_head = grad_mixed[:, part * HEAD_DIM : (part + 1) * HEAD_DIM].astype(BF16)
            x_head = x_ref[:, cols].astype(F32)
            normed = x_head * inverse
            queries = (normed * gq_ref[:, cols]).astype(BF16)
            keys = (normed * gk_ref[:, cols]).astype(BF16)
            values = (normed * gv_ref[:, cols]).astype(BF16)
            probs = probs_buf[head]
            grad_values = dot(probs.astype(BF16), grad_head, TN)
            weighted = probs * dot(grad_head, values, NT)
            grad_scores = weighted - probs * jnp.sum(weighted, axis=1, keepdims=True)
            grad_scores = (grad_scores * scale).astype(BF16)
            grad_queries = dot(grad_scores, keys, NN)
            grad_keys = dot(grad_scores, queries, TN)
            grad_normed = (
                grad_queries * gq_ref[:, cols]
                + grad_keys * gk_ref[:, cols]
                + grad_values * gv_ref[:, cols]
            )
            inner = inner + grad_normed * x_head
            sum_ref[:, cols] = grad_ref[:, cols].astype(F32) + grad_normed * inverse
    inner_ref[...] = jnp.sum(inner, axis=1, keepdims=True)


VMEM = pl.BlockSpec(memory_space=pltpu.VMEM)
SMEM = pl.BlockSpec(memory_space=pltpu.SMEM)
ANY = pl.BlockSpec(memory_space=pl.ANY)


def forward_call(rows, width):
    full = 2 * width
    shape = jax.ShapeDtypeStruct((rows, width), BF16)
    return pl.pallas_call(
        forward_kernel,
        out_shape=(shape, shape, shape),
        in_specs=[SMEM] + [VMEM] * 7 + [ANY],
        out_specs=(VMEM, VMEM, VMEM),
        scratch_shapes=[
            pltpu.VMEM((full, width), BF16),
            pltpu.SemaphoreType.DMA((full // CHUNK,)),
        ],
        compiler_params=pltpu.CompilerParams(vmem_limit_bytes=VMEM_LIMIT),
        name="layer_forward",
    )


def backward_call(rows, width):
    full = 2 * width
    return pl.pallas_call(
        backward_kernel,
        out_shape=(
            jax.ShapeDtypeStruct((rows, width), F32),
            jax.ShapeDtypeStruct((rows, 1), F32),
        ),
        in_specs=[SMEM] + [VMEM] * 7 + [ANY] + [VMEM] * 2,
        out_specs=(VMEM, VMEM),
        scratch_shapes=[
            pltpu.VMEM((full, width), BF16),
            pltpu.VMEM((width // HEAD_DIM, rows, rows), F32),
            pltpu.SemaphoreType.DMA((full // CHUNK,)),
        ],
        compiler_params=pltpu.CompilerParams(vmem_limit_bytes=VMEM_LIMIT),
        name="layer_backward",
    )


def local(tokens_in, query_gain, key_gain, value_gain, out_weight, doc_lengths, grad_out):
    rows, width = tokens_in.shape
    full = 2 * width
    sections = lax.axis_size("section")
    shards = lax.axis_size("dp")
    section = lax.axis_index("section")
    half = lax.axis_index("tensor").astype(jnp.int32).reshape(1)

    def swap(block):
        return lax.ppermute(block, "tensor", [(0, 1), (1, 0)])

    def relay(block, step):
        route = [(i, i + step) for i in range(sections) if 0 <= i + step < sections]
        return lax.ppermute(block, "section", route)

    ends = jnp.cumsum(doc_lengths[0])
    ident = jnp.sum(
        (jnp.arange(rows, dtype=jnp.int32)[:, None] >= ends[None, :]).astype(jnp.int32), axis=1
    )
    id_col, id_row = ident[:, None], ident[None, :]
    gains = (query_gain, key_gain, value_gain)
    weight = lax.all_gather(out_weight[0].T, "dp", axis=0, tiled=True)

    def row_squares(block):
        wide = block.astype(F32)
        own = jnp.sum(wide * wide, axis=1, keepdims=True)
        return own + swap(own)

    first_squares = row_squares(tokens_in)
    forward = forward_call(rows, width)
    x, squares = tokens_in, first_squares
    for turn in range(sections):
        own, other, mixed = forward(half, x, squares, *gains, id_col, id_row, weight)
        total = own.astype(F32) + swap(other).astype(F32)
        output = (x.astype(F32) + total).astype(BF16)
        if turn < sections - 1:
            arrived = relay(output, 1)
            arrived_squares = relay(row_squares(output), 1)
            x = jnp.where(section == 0, tokens_in, arrived)
            squares = jnp.where(section == 0, first_squares, arrived_squares)

    mixed_all = lax.all_gather(mixed, "dp", axis=0)

    backward = backward_call(rows, width)
    inverse = lax.rsqrt(squares / full + EPS)
    x_wide = x.astype(F32)
    grad = grad_out
    for turn in range(sections):
        grad_other = swap(grad)
        pulled, inner = backward(
            half, x, squares, *gains, id_col, id_row, weight, grad, grad_other
        )
        inner = inner + swap(inner)
        grad_in = (pulled - x_wide * (inner * inverse * inverse * inverse / full)).astype(BF16)
        if turn < sections - 1:
            arrived = relay(grad_in, -1)
            grad = jnp.where(section == sections - 1, grad_out, arrived)

    first = jnp.where(half[0] == 0, grad, grad_other)
    second = jnp.where(half[0] == 0, grad_other, grad)
    columns = jnp.concatenate([first.T, second.T], axis=0).reshape(shards, full // shards, rows)
    columns = lax.all_to_all(columns, "dp", split_axis=0, concat_axis=0)
    weight_grads = lax.dot_general(
        mixed_all, columns, (((0, 1), (0, 2)), ((), ())), preferred_element_type=F32
    )
    return output[None], grad_in[None], weight_grads[None]


def solution(mesh):
    return jax.shard_map(
        local,
        mesh=mesh,
        in_specs=(
            P("dp", "tensor"),
            P("section", "tensor"),
            P("section", "tensor"),
            P("section", "tensor"),
            P("section", "tensor", "dp"),
            P("dp", None),
            P("dp", "tensor"),
        ),
        out_specs=(
            P("section", "dp", "tensor"),
            P("section", "dp", "tensor"),
            P("section", "tensor", "dp"),
        ),
        check_vma=False,
    )
```

time: 1990 us -> 608 us (0.31)
  waiting for transfers between devices: 928 us -> 429 us
  local copies, waits for them, and re-layouts: 426 us -> 4.97 us
  matrix products: 280 us -> 7.31 us
  other arithmetic: 189 us -> 5.78 us
  Pallas kernels: 0 us -> 105 us
  blocking collectives: 75 us -> 0 us
  starting transfers between devices: 59.1 us -> 31.7 us
    reduce_scatter x12 -> x0, waiting for transfers between devices: 701 us -> none  [the longest x1 555 us: local(): lax.psum_scatter(weight_term.astype(jnp.bfloat16), 'dp', scatter_dimensio...]
    dot_general x100 -> x1, matrix products: 280 us -> 7.31 us  [local(): lax.dot_general(mixed_all, columns, (((0, 1), (0, 2)), ((), ())), preferr...]
    select_n x88 -> x0, local copies, waits for them, and re-layouts: 265 us -> none  [place(): jnp.where(is_valid, lax.dynamic_update_slice_in_dim(buffer, piece, row_st...]
    ppermute x22 -> x25, waiting for transfers between devices: 23.4 us -> 191 us  [the longest x9 170 us: relay(): return lax.ppermute(block, 'section', route)]
    while x124 -> x0, local copies, waits for them, and re-layouts: 112 us -> none
    pallas_call x0 -> x8, Pallas kernels: none -> 105 us  [the longest x4 57 us: local(): forward(half, x, squares, *gains, id_col, id_row, weight)]
    psum x22 -> x0, blocking collectives: 54.2 us -> none  [the longest x11 27.1 us: forward_turn(): squares = lax.psum(jnp.sum(group_f * group_f, axis=1), 'tensor')]
    select_n x77 -> x9, other arithmetic: 46 us -> 0.32 us  [the longest x3 0.15 us: local(): x = jnp.where(section == 0, tokens_in, arrived)]
  transfers between devices with their start and end apart: 35 -> 28, of which waited for: 24 -> 24; matrix products, arithmetic and copies ran while one was open for 11% -> 1% of each run, Pallas kernels for 0% -> 8%
where the time goes in v1:
time: 608 us; the launch traced here: 599 us
  waiting for transfers between devices  429 us (71%)
  Pallas kernels  105 us (17%)
  starting transfers between devices  31.7 us (5%)
  between operations  15 us (2%)
  matrix products  7.31 us (1%)
    all_gather x1, waiting for transfers between devices, local(): weight = lax.all_gather(out_weight[0].T, 'dp', axis=0, tiled=True)  204 us
    ppermute x9, waiting for transfers between devices, relay(): return lax.ppermute(block, 'section', route)  170 us
    pallas_call x4, Pallas kernels, local(): forward(half, x, squares, *gains, id_col, id_row, weight)  57 us
    pallas_call x4, Pallas kernels, local(): backward(half, x, squares, *gains, id_col, id_row, weight, grad, grad_other)  47.8 us
    ppermute x16, waiting for transfers between devices, swap(): return lax.ppermute(block, 'tensor', [(0, 1), (1, 0)])  21 us
    ppermute x9, starting transfers between devices, relay(): return lax.ppermute(block, 'section', route)  19.1 us
    all_gather x1, waiting for transfers between devices, local(): mixed_all = lax.all_gather(mixed, 'dp', axis=0)  17.1 us
    all_to_all x1, waiting for transfers between devices, local(): columns = lax.all_to_all(columns, 'dp', split_axis=0, concat_axis=0)  16.1 us
  transfers between devices with their start and end apart: 28, of which 24 were waited for; matrix products, arithmetic and copies ran while one was open for 1% of the time, Pallas kernels for 8%

profile of v1, /device:TPU:32, one launch (start us, length us, event | category | flops | bytes accessed | tf_op | source)
XLA Modules:
  0.0 598.8 jit_solution(4446315067087505796)
XLA Ops:
  8.0 1.2 fusion
  9.4 0.8 reduce-window.8
  10.7 204.0 %all-gather.4.cloned.1.call-done.weight_ref = bf16[3584,1792]{1,0:T(8,128)(2,1)} async-done(((bf16[112,1792]{1,0:T(8,128)(2,1)}), bf16[3584,1792]{1,0:T(8,128)(2,1)}) %all-gather.4.cloned.1.call-update) | async-done | bytes 12845072 | tf_op jit(solution)/shard_map/all_gather | solution.py:202
  214.7 1.0 copy-done
  215.7 0.7 copy-done.3
  217.8 14.3 %layer_forward.4 = (bf16[128,1792]{1,0:T(8,128)(2,1)S(1)}, bf16[128,1792]{1,0:T(8,128)(2,1)S(1)}, bf16[128,1792]{1,0:T(8,128)(2,1)}) custom-call(s32[1]{0:T(128)} %bitcast.half_ref, bf16[128,1792]{1,0:T(8,128)(2,1)S(1)} %copy-done, f32[128,1]{1,0:T(8,128)S(1)} %add.54.squares_ref, f32[1,1792]{1,0:T(1,128)S(1)} %copy-done.3, f32[1,1792]{1,0:T(1,128)S(1)} %copy-done.5, ...), custom_call_target="tpu_custom_call" | custom-call | tf_op jit(solution)/shard_map/layer_forward/pallas_call | solution.py:213
  232.1 1.8 collective-permute-done.1
  234.2 2.3 collective-permute-start.2
  236.8 1.2 collective-permute-done.3
  238.0 1.9 collective-permute-start.4
  240.0 10.1 %collective-permute-done.4 = f32[128,1]{1,0:T(8,128)S(1)} collective-permute-done((f32[128,1]{1,0:T(8,128)S(1)}, f32[128,1]{1,0:T(8,128)S(1)}, u32[]{:S(2)}, u32[]{:S(2)}) %collective-permute-start.4) | collective-permute-done | bytes 544 | tf_op jit(solution)/shard_map/ppermute | solution.py:194
  250.2 14.3 %layer_forward.5 = (bf16[128,1792]{1,0:T(8,128)(2,1)S(1)}, bf16[128,1792]{1,0:T(8,128)(2,1)S(1)}, bf16[128,1792]{1,0:T(8,128)(2,1)}) custom-call(s32[1]{0:T(128)} %bitcast.half_ref, bf16[128,1792]{1,0:T(8,128)(2,1)S(1)} %broadcast_select_fusion.5.x_ref, f32[128,1]{1,0:T(8,128)S(1)} %broadcast_select_fusion.8.squares_ref, f32[1,1792]{1,0:T(1,128)S(1)} %copy-done.4, ...), custom_call_target="tpu_custom_call" | custom-call | tf_op jit(solution)/shard_map/layer_forward/pallas_call | solution.py:213
  264.9 1.8 collective-permute-done.5
  267.1 2.3 collective-permute-start.6
  269.6 1.2 collective-permute-done.7
  270.9 2.2 collective-permute-start.8
  273.1 9.9 %collective-permute-done.8 = f32[128,1]{1,0:T(8,128)S(1)} collective-permute-done((f32[128,1]{1,0:T(8,128)S(1)}, f32[128,1]{1,0:T(8,128)S(1)}, u32[]{:S(2)}, u32[]{:S(2)}) %collective-permute-start.8) | collective-permute-done | bytes 544 | tf_op jit(solution)/shard_map/ppermute | solution.py:194
  283.0 14.3 %layer_forward.6 = (bf16[128,1792]{1,0:T(8,128)(2,1)S(1)}, bf16[128,1792]{1,0:T(8,128)(2,1)S(1)}, bf16[128,1792]{1,0:T(8,128)(2,1)}) custom-call(s32[1]{0:T(128)} %bitcast.half_ref, bf16[128,1792]{1,0:T(8,128)(2,1)S(1)} %broadcast_select_fusion.4.x_ref, f32[128,1]{1,0:T(8,128)S(1)} %broadcast_select_fusion.7.squares_ref, f32[1,1792]{1,0:T(1,128)S(1)} %copy-done.4, ...), custom_call_target="tpu_custom_call" | custom-call | tf_op jit(solution)/shard_map/layer_forward/pallas_call | solution.py:213
  297.4 1.8 collective-permute-done.9
  299.5 2.3 collective-permute-start.10
  302.0 1.2 collective-permute-done.11
  303.3 2.2 collective-permute-start.12
  305.5 9.9 %collective-permute-done.12 = f32[128,1]{1,0:T(8,128)S(1)} collective-permute-done((f32[128,1]{1,0:T(8,128)S(1)}, f32[128,1]{1,0:T(8,128)S(1)}, u32[]{:S(2)}, u32[]{:S(2)}) %collective-permute-start.12) | collective-permute-done | bytes 544 | tf_op jit(solution)/shard_map/ppermute | solution.py:194
  315.4 14.3 %layer_forward.7 = (bf16[128,1792]{1,0:T(8,128)(2,1)S(1)}, bf16[128,1792]{1,0:T(8,128)(2,1)S(1)}, bf16[128,1792]{1,0:T(8,128)(2,1)}) custom-call(s32[1]{0:T(128)} %bitcast.half_ref, bf16[128,1792]{1,0:T(8,128)(2,1)S(1)} %broadcast_select_fusion.3.x_ref, f32[128,1]{1,0:T(8,128)S(1)} %broadcast_select_fusion.6.squares_ref, f32[1,1792]{1,0:T(1,128)S(1)} %copy-done.4, ...), custom_call_target="tpu_custom_call" | custom-call | tf_op jit(solution)/shard_map/layer_forward/pallas_call | solution.py:213
  330.0 1.8 collective-permute-done.14.grad_other_ref
  331.8 11.9 %layer_backward.4 = (f32[128,1792]{1,0:T(8,128)S(1)}, f32[128,1]{1,0:T(8,128)S(1)}) custom-call(s32[1]{0:T(128)} %bitcast.half_ref, bf16[128,1792]{1,0:T(8,128)(2,1)S(1)} %broadcast_select_fusion.3.x_ref, f32[128,1]{1,0:T(8,128)S(1)} %broadcast_select_fusion.6.squares_ref, f32[1,1792]{1,0:T(1,128)S(1)} %copy-done.4, f32[1,1792]{1,0:T(1,128)S(1)} %copy-done.6, ...), custom_call_target="tpu_custom_call" | custom-call | tf_op jit(solution)/shard_map/layer_backward/pallas_call | solution.py:230
  343.9 1.1 collective-permute-done.15
  345.3 1.9 collective-permute-start.16
  347.3 13.5 %collective-permute-done.16 = bf16[128,1792]{1,0:T(8,128)(2,1)S(1)} collective-permute-done((bf16[128,1792]{1,0:T(8,128)(2,1)S(1)}, bf16[128,1792]{1,0:T(8,128)(2,1)S(1)}, u32[]{:S(2)}, u32[]{:S(2)}) %collective-permute-start.16) | collective-permute-done | bytes 458784 | tf_op jit(solution)/shard_map/ppermute | solution.py:194
  360.9 1.8 collective-permute-done.17.grad_other_ref
  362.7 12.0 %layer_backward.5 = (f32[128,1792]{1,0:T(8,128)S(1)}, f32[128,1]{1,0:T(8,128)S(1)}) custom-call(s32[1]{0:T(128)} %bitcast.half_ref, bf16[128,1792]{1,0:T(8,128)(2,1)S(1)} %broadcast_select_fusion.3.x_ref, f32[128,1]{1,0:T(8,128)S(1)} %broadcast_select_fusion.6.squares_ref, f32[1,1792]{1,0:T(1,128)S(1)} %copy-done.4, f32[1,1792]{1,0:T(1,128)S(1)} %copy-done.6, ...), custom_call_target="tpu_custom_call" | custom-call | tf_op jit(solution)/shard_map/layer_backward/pallas_call | solution.py:230
  375.1 1.2 collective-permute-done.18
  376.6 1.9 collective-permute-start.19
  378.5 27.0 %collective-permute-done.19 = bf16[128,1792]{1,0:T(8,128)(2,1)S(1)} collective-permute-done((bf16[128,1792]{1,0:T(8,128)(2,1)S(1)}, bf16[128,1792]{1,0:T(8,128)(2,1)S(1)}, u32[]{:S(2)}, u32[]{:S(2)}) %collective-permute-start.19) | collective-permute-done | bytes 458784 | tf_op jit(solution)/shard_map/ppermute | solution.py:194
  405.7 1.8 collective-permute-done.20.grad_other_ref
  407.5 12.1 %layer_backward.6 = (f32[128,1792]{1,0:T(8,128)S(1)}, f32[128,1]{1,0:T(8,128)S(1)}) custom-call(s32[1]{0:T(128)} %bitcast.half_ref, bf16[128,1792]{1,0:T(8,128)(2,1)S(1)} %broadcast_select_fusion.3.x_ref, f32[128,1]{1,0:T(8,128)S(1)} %broadcast_select_fusion.6.squares_ref, f32[1,1792]{1,0:T(1,128)S(1)} %copy-done.4, f32[1,1792]{1,0:T(1,128)S(1)} %copy-done.6, ...), custom_call_target="tpu_custom_call" | custom-call | tf_op jit(solution)/shard_map/layer_backward/pallas_call | solution.py:230
  419.7 1.2 collective-permute-done.21
  421.3 1.9 collective-permute-start.22
  423.2 99.9 %collective-permute-done.22 = bf16[128,1792]{1,0:T(8,128)(2,1)S(1)} collective-permute-done((bf16[128,1792]{1,0:T(8,128)(2,1)S(1)}, bf16[128,1792]{1,0:T(8,128)(2,1)S(1)}, u32[]{:S(2)}, u32[]{:S(2)}) %collective-permute-start.22) | collective-permute-done | bytes 458784 | tf_op jit(solution)/shard_map/ppermute | solution.py:194
  523.3 1.8 collective-permute-done.23.grad_other_ref
  525.2 1.3 copy.60
  526.5 9.4 %all-to-all-start = ((bf16[32,112,128]{2,1,0:T(8,128)(2,1)}), bf16[32,112,128]{2,1,0:T(8,128)(2,1)S(1)}, u32[]{:S(2)}, u32[]{:S(2)}) async-start(bf16[32,112,128]{2,1,0:T(8,128)(2,1)} %bitcast.37), calls=%async_computation | async-start | bytes 1835008 | tf_op jit(solution)/shard_map/all_to_all | solution.py:242
  536.2 11.9 %layer_backward.7 = (f32[128,1792]{1,0:T(8,128)S(1)}, f32[128,1]{1,0:T(8,128)S(1)}) custom-call(s32[1]{0:T(128)} %bitcast.half_ref, bf16[128,1792]{1,0:T(8,128)(2,1)S(1)} %broadcast_select_fusion.3.x_ref, f32[128,1]{1,0:T(8,128)S(1)} %broadcast_select_fusion.6.squares_ref, f32[1,1792]{1,0:T(1,128)S(1)} %copy-done.4, f32[1,1792]{1,0:T(1,128)S(1)} %copy-done.6, ...), custom_call_target="tpu_custom_call" | custom-call | tf_op jit(solution)/shard_map/layer_backward/pallas_call | solution.py:230
  548.7 0.9 collective-permute-done.24
  549.7 1.2 fusion.11
  550.9 16.1 %all-to-all-done = bf16[32,112,128]{2,1,0:T(8,128)(2,1)S(1)} async-done(((bf16[32,112,128]{2,1,0:T(8,128)(2,1)}), bf16[32,112,128]{2,1,0:T(8,128)(2,1)S(1)}, u32[]{:S(2)}, u32[]{:S(2)}) %all-to-all-start) | async-done | bytes 917536 | tf_op jit(solution)/shard_map/all_to_all | solution.py:242
  567.0 17.1 %all-gather.6.cloned.1.call-done = bf16[4096,1792]{1,0:T(8,128)(2,1)} async-done(((bf16[128,1792]{1,0:T(8,128)(2,1)}), bf16[4096,1792]{1,0:T(8,128)(2,1)}) %all-gather.6.cloned.1.call-update) | async-done | bytes 14680080 | tf_op jit(solution)/shard_map/all_gather | solution.py:222
  584.2 7.3 %convolution_bitcast_fusion = f32[1,1792,112]{1,2,0:T(8,128)} fusion(bf16[32,112,128]{2,1,0:T(8,128)(2,1)S(1)} %all-to-all-done, bf16[32,128,1792]{2,1,0:T(8,128)(2,1)} %bitcast.36), kind=kOutput, calls=%fused_computation | convolution fusion | flops 1644167168 | bytes 16400384 | tf_op jit(solution)/shard_map/dot_general | solution.py:243
  (72 shorter events, 8.7 us)
Async XLA Ops:
  7.2 243.0 %copy-start.1 = (bf16[128,1792]{1,0:T(8,128)(2,1)S(1)}, bf16[128,1792]{1,0:T(8,128)(2,1)}, u32[]{:S(2)}) copy-start(bf16[128,1792]{1,0:T(8,128)(2,1)} %x_ref.1) | copy-start | bytes 1376260
  7.2 243.0 %copy-start.4 = (f32[1,1792]{1,0:T(1,128)S(1)}, f32[1,1792]{1,0:T(1,128)}, u32[]{:S(2)}) copy-start(f32[1,1792]{1,0:T(1,128)} %gq_ref.15) | copy-start | bytes 21508
  7.2 243.0 %copy-start.6 = (f32[1,1792]{1,0:T(1,128)S(1)}, f32[1,1792]{1,0:T(1,128)}, u32[]{:S(2)}) copy-start(f32[1,1792]{1,0:T(1,128)} %gk_ref.15) | copy-start | bytes 21508
  7.2 243.0 %copy-start.8 = (f32[1,1792]{1,0:T(1,128)S(1)}, f32[1,1792]{1,0:T(1,128)}, u32[]{:S(2)}) copy-start(f32[1,1792]{1,0:T(1,128)} %gv_ref.15) | copy-start | bytes 21508
  7.2 207.5 %all-gather.4.cloned.1.call-start = ((), (), s32[]{:S(2)}) async-start(), calls=%async_computation.1 | async-start | bytes 13246464 | tf_op jit(solution)/shard_map/all_gather | solution.py:202
  7.9 576.2 %all-gather.6.cloned.1.call-start = ((), (), s32[]{:S(2)}) async-start(), calls=%async_computation.2 | async-start | bytes 15138816 | tf_op jit(solution)/shard_map/all_gather | solution.py:222
  9.3 1.3 collective-permute-start
  214.7 1.0 copy-start
  215.7 0.7 copy-start.3
  216.4 0.7 copy-start.5
  217.1 0.7 copy-start.7
  232.0 1.9 collective-permute-start.1
  234.2 15.9 %collective-permute-start.2 = (bf16[128,1792]{1,0:T(8,128)(2,1)S(1)}, bf16[128,1792]{1,0:T(8,128)(2,1)S(1)}, u32[]{:S(2)}, u32[]{:S(2)}) collective-permute-start(bf16[128,1792]{1,0:T(8,128)(2,1)S(1)} %get-tuple-element.42), channel_id=1, source_target_pairs={{0,2},{2,4},{4,6},{1,3},{3,5},{5,7},{8,10},{10,12},{12,14},{9,11},... | collective-permute-start | bytes 1376264 | tf_op jit(solution)/shard_map/ppermute | solution.py:194
  236.7 1.3 collective-permute-start.3
  238.0 12.1 %collective-permute-start.4 = (f32[128,1]{1,0:T(8,128)S(1)}, f32[128,1]{1,0:T(8,128)S(1)}, u32[]{:S(2)}, u32[]{:S(2)}) collective-permute-start(f32[128,1]{1,0:T(8,128)S(1)} %add.57), channel_id=1, source_target_pairs={{0,2},{2,4},{4,6},{1,3},{3,5},{5,7},{8,10},{10,12},{12,14},{9,11},... | collective-permute-start | bytes 1544 | tf_op jit(solution)/shard_map/ppermute | solution.py:194
  264.5 2.2 collective-permute-start.5
  267.1 15.9 %collective-permute-start.6 = (bf16[128,1792]{1,0:T(8,128)(2,1)S(1)}, bf16[128,1792]{1,0:T(8,128)(2,1)S(1)}, u32[]{:S(2)}, u32[]{:S(2)}) collective-permute-start(bf16[128,1792]{1,0:T(8,128)(2,1)S(1)} %get-tuple-element.40), channel_id=1, source_target_pairs={{0,2},{2,4},{4,6},{1,3},{3,5},{5,7},{8,10},{10,12},{12,14},{9,11},... | collective-permute-start | bytes 1376264 | tf_op jit(solution)/shard_map/ppermute | solution.py:194
  269.5 1.3 collective-permute-start.7
  270.9 12.1 %collective-permute-start.8 = (f32[128,1]{1,0:T(8,128)S(1)}, f32[128,1]{1,0:T(8,128)S(1)}, u32[]{:S(2)}, u32[]{:S(2)}) collective-permute-start(f32[128,1]{1,0:T(8,128)S(1)} %add.60), channel_id=1, source_target_pairs={{0,2},{2,4},{4,6},{1,3},{3,5},{5,7},{8,10},{10,12},{12,14},{9,11},... | collective-permute-start | bytes 1544 | tf_op jit(solution)/shard_map/ppermute | solution.py:194
  283.0 46.7 %copy-start.2 = (bf16[128,1792]{1,0:T(8,128)(2,1)S(1)}, bf16[128,1792]{1,0:T(8,128)(2,1)}, u32[]{:S(2)}) copy-start(bf16[128,1792]{1,0:T(8,128)(2,1)} %grad_ref.1) | copy-start | bytes 1376260
  297.3 1.9 collective-permute-start.9
  299.5 15.9 %collective-permute-start.10 = (bf16[128,1792]{1,0:T(8,128)(2,1)S(1)}, bf16[128,1792]{1,0:T(8,128)(2,1)S(1)}, u32[]{:S(2)}, u32[]{:S(2)}) collective-permute-start(bf16[128,1792]{1,0:T(8,128)(2,1)S(1)} %get-tuple-element.38), channel_id=1, source_target_pairs={{0,2},{2,4},{4,6},{1,3},{3,5},{5,7},{8,10},{10,12},{12,14},{9,11},... | collective-permute-start | bytes 1376264 | tf_op jit(solution)/shard_map/ppermute | solution.py:194
  301.9 1.3 collective-permute-start.11
  303.3 12.1 %collective-permute-start.12 = (f32[128,1]{1,0:T(8,128)S(1)}, f32[128,1]{1,0:T(8,128)S(1)}, u32[]{:S(2)}, u32[]{:S(2)}) collective-permute-start(f32[128,1]{1,0:T(8,128)S(1)} %add.63), channel_id=1, source_target_pairs={{0,2},{2,4},{4,6},{1,3},{3,5},{5,7},{8,10},{10,12},{12,14},{9,11},... | collective-permute-start | bytes 1544 | tf_op jit(solution)/shard_map/ppermute | solution.py:194
  329.7 2.1 collective-permute-start.14
  343.7 1.3 collective-permute-start.15
  345.3 15.4 %collective-permute-start.16 = (bf16[128,1792]{1,0:T(8,128)(2,1)S(1)}, bf16[128,1792]{1,0:T(8,128)(2,1)S(1)}, u32[]{:S(2)}, u32[]{:S(2)}) collective-permute-start(bf16[128,1792]{1,0:T(8,128)(2,1)S(1)} %fusion.4), channel_id=1, source_target_pairs={{2,0},{4,2},{6,4},{3,1},{5,3},{7,5},{10,8},{12,10},{14,12},{11,9},... | collective-permute-start | bytes 1376264 | tf_op jit(solution)/shard_map/ppermute | solution.py:194
  360.8 1.9 collective-permute-start.17
  374.7 1.6 collective-permute-start.18
  376.6 29.0 %collective-permute-start.19 = (bf16[128,1792]{1,0:T(8,128)(2,1)S(1)}, bf16[128,1792]{1,0:T(8,128)(2,1)S(1)}, u32[]{:S(2)}, u32[]{:S(2)}) collective-permute-start(bf16[128,1792]{1,0:T(8,128)(2,1)S(1)} %fusion.6), channel_id=1, source_target_pairs={{2,0},{4,2},{6,4},{3,1},{5,3},{7,5},{10,8},{12,10},{14,12},{11,9},... | collective-permute-start | bytes 1376264 | tf_op jit(solution)/shard_map/ppermute | solution.py:194
  405.6 1.9 collective-permute-start.20
  419.6 1.3 collective-permute-start.21
  421.3 101.8 %collective-permute-start.22 = (bf16[128,1792]{1,0:T(8,128)(2,1)S(1)}, bf16[128,1792]{1,0:T(8,128)(2,1)S(1)}, u32[]{:S(2)}, u32[]{:S(2)}) collective-permute-start(bf16[128,1792]{1,0:T(8,128)(2,1)S(1)} %fusion.8), channel_id=1, source_target_pairs={{2,0},{4,2},{6,4},{3,1},{5,3},{7,5},{10,8},{12,10},{14,12},{11,9},... | collective-permute-start | bytes 1376264 | tf_op jit(solution)/shard_map/ppermute | solution.py:194
  523.2 1.9 collective-permute-start.23
  526.5 40.6 %all-to-all-start = ((bf16[32,112,128]{2,1,0:T(8,128)(2,1)}), bf16[32,112,128]{2,1,0:T(8,128)(2,1)S(1)}, u32[]{:S(2)}, u32[]{:S(2)}) async-start(bf16[32,112,128]{2,1,0:T(8,128)(2,1)} %bitcast.37), calls=%async_computation | async-start | bytes 1835008 | tf_op jit(solution)/shard_map/all_to_all | solution.py:242
  535.9 13.8 %collective-permute-start.13 = (bf16[128,1792]{1,0:T(8,128)(2,1)S(1)}, bf16[128,1792]{1,0:T(8,128)(2,1)S(1)}, u32[]{:S(2)}, u32[]{:S(2)}) collective-permute-start(bf16[128,1792]{1,0:T(8,128)(2,1)S(1)} %get-tuple-element.27), channel_id=1, source_target_pairs={{0,1},{1,0},{2,3},{3,2},{4,5},{5,4},{6,7},{7,6},{8,9},{9,8},{10,11... | collective-permute-start | bytes 1376264 | tf_op jit(solution)/shard_map/ppermute | solution.py:190
  548.1 1.5 collective-permute-start.24
Sparse Core Ops, SparseCore 0:
  11.5 203.1 all-gather.3
  329.9 254.2 all-gather.5
